TPU v7x, 32 devices: a whole 2x2x4 slice. The times are simulated.
32 devices in a mesh: grp: 8 (over y, x, core), seq: 4 (over z).
Axes of the slice: x: 2, y: 2, z: 4, core: 2. Of those that a mesh axis runs over, the one named last changes fastest.
Arguments:
- lengths: int32 [16], replicated, may hold values from 42 to 1024, as said below
- group_of: int32 [16], replicated, may hold values from 0 to 7, as said below
- query_pre: bfloat16 [8192, 8192], P(('grp', 'seq')), may hold values from -170 to 170
- key_pre: bfloat16 [8192, 1024], P(('grp', 'seq')), may hold values from -7 to 7
- value_pre: bfloat16 [8192, 1024], P(('grp', 'seq')), may hold values from -4 to 4
- query_new: bfloat16 [16, 8192], P(None, 'seq'), may hold values from -170 to 170
- key_new: bfloat16 [16, 1024], P(None, 'seq'), may hold values from -4 to 4
- value_new: bfloat16 [16, 1024], P(None, 'seq'), may hold values from -4 to 4
- hidden_new: bfloat16 [16, 8192], P(None, 'grp'), may hold values from -3 to 3
- out_weight: bfloat16 [8192, 8192], P('seq', 'grp'), may hold values from -0.0625 to 0.0625
- norm_gain: bfloat16 [8192], P('grp'), may hold values from 0.099609375 to 1.8984375
- gate_weight: bfloat16 [8192, 16384], P('grp', 'seq'), may hold values from -0.0625 to 0.0625
- up_weight: bfloat16 [8192, 16384], P('grp', 'seq'), may hold values from -0.0625 to 0.0625
- down_weight: bfloat16 [16384, 8192], P('seq', 'grp'), may hold values from -0.046875 to 0.046875
Outputs:
- prefill_attention: bfloat16 [8192, 8192], P(('grp', 'seq'))
- decode_hidden: bfloat16 [16, 8192], P(None, ('grp', 'seq'))
Inputs may be any that keep to these rules, and one draw needn't show every extreme that they name: Two requests have length exactly 1024 and are alone in their groups; the others have lengths from 42 to 341; the lengths in one group sum to at most 1024. `group_of`: every group holds at least one request and at most three.
All inputs are finite; a program needn't handle non-finite values.
Results may differ from a plain program's by a relative error of at most 0.0095.
Values may be sent and summed in bfloat16 or wider, within the bound.
No kernel may reach another device: no remote copies, remote signals or barrier semaphores. Data moves between devices by JAX's collectives and lax.ppermute only.
A program may use at most 320 MiB of HBM per device.

v0:
```python
import functools
import math

import jax
import jax.numpy as jnp
from jax import lax
from jax.experimental import pallas as pl
from jax.experimental.pallas import tpu as pltpu
from jax.sharding import PartitionSpec as P

HD = 128
Q_PER_KV = 8
MAX_IN_GROUP = 3
SLOTS_R = 4
NEGATIVE = -1e30
LOG2E = 1.4426950408889634
MIB = 1 << 20
STREAM = 57

F32 = jnp.float32
BF16 = jnp.bfloat16


def dot(a, b):
    return jnp.dot(a, b, preferred_element_type=F32)


def dot_t(a, b):
    return lax.dot_general(a, b, (((1,), (1,)), ((), ())), preferred_element_type=F32)


def plan(facts):
    group = facts[0]
    reqs = (facts.shape[0] - 2) // 2
    ids = [jnp.int32(-1)] * MAX_IN_GROUP
    first = [jnp.int32(0)] * MAX_IN_GROUP
    end = [jnp.int32(0)] * MAX_IN_GROUP
    count = jnp.int32(0)
    used = jnp.int32(0)
    for r in range(reqs):
        mine = facts[2 + r] == group
        length = facts[2 + reqs + r]
        for k in range(MAX_IN_GROUP):
            here = mine & (count == k)
            ids[k] = jnp.where(here, r, ids[k])
            first[k] = jnp.where(here, used, first[k])
            end[k] = jnp.where(here, used + length, end[k])
        count = count + jnp.where(mine, 1, 0)
        used = used + jnp.where(mine, length, 0)
    return ids, first, end


def pick_rows(ids, rows, columns):
    row = lax.broadcasted_iota(jnp.int32, (rows, columns), 0)
    column = lax.broadcasted_iota(jnp.int32, (rows, columns), 1)
    target = jnp.full((rows, columns), -1, jnp.int32)
    for k in range(MAX_IN_GROUP):
        target = jnp.where(row == k, ids[k], target)
    return jnp.where(column == target, 1.0, 0.0).astype(BF16)


def split3(x):
    hi = x.astype(BF16)
    rest = x - hi.astype(F32)
    mid = rest.astype(BF16)
    low = (rest - mid.astype(F32)).astype(BF16)
    return hi, mid, low


def by_head(array, group):
    heads = array.shape[1] // HD * group
    return jnp.concatenate([array[:, (h // group) * HD :][:, :HD] for h in range(heads)], axis=0)


def spread(x, lane):
    hi, mid, low = split3(jnp.broadcast_to(x, x.shape[:-1] + (HD,)))
    return jnp.where(
        lane < 32, hi.astype(F32), jnp.where(lane < 64, mid.astype(F32), low.astype(F32))
    ).astype(BF16)


def gathered(stats):
    return stats[..., 0:1] + stats[..., 32:33] + stats[..., 64:65]


def select_kernel(facts, new_ref, query_ref, own_ref):
    ids, _, _ = plan(facts)
    width = query_ref.shape[1]
    kv_width = (new_ref.shape[1] - width) // 2
    new = dot(pick_rows(ids, 8, new_ref.shape[0]), new_ref[...])[:SLOTS_R]
    query_ref[...] = new[:, :width].astype(BF16)
    keys = by_head(new[:, width : width + kv_width], Q_PER_KV)
    values = by_head(new[:, width + kv_width :], Q_PER_KV)
    score = jnp.sum(by_head(new[:, :width], 1) * keys, axis=1, keepdims=True)
    own_ref[:, :HD] = values
    own_ref[:, HD:] = jnp.broadcast_to(score * (1.0 / math.sqrt(HD)), values.shape)


def pack_kernel(key_ref, value_ref, out_ref):
    tokens, width = key_ref.shape
    for at in range(0, width, HD):
        keys = key_ref[:, at : at + HD].astype(F32)
        out_ref[at : at + HD, :] = jnp.transpose(keys).astype(BF16)
    for at in range(0, width, tokens):
        out_ref[width + at : width + at + tokens, :] = value_ref[:, at : at + tokens]


def value_place(kv, tokens):
    side = tokens // HD
    row = pl.multiple_of(kv // side * tokens, tokens)
    return row, pl.multiple_of(lax.rem(kv, side) * HD, HD)


def partial_kernel(n, facts, *refs):
    queries, cache_ref, outs = refs[:n], refs[n], refs[n + 1 : 2 * n + 1]
    query_ref, out_ref = refs[2 * n + 1 :]
    _, first, end = plan(facts)
    kv_width, tokens = cache_ref.shape[0] // 2, cache_ref.shape[1]
    kv_per = queries[0].shape[1] // (HD * Q_PER_KV)
    rows = Q_PER_KV * SLOTS_R
    slot = facts[1] * tokens + lax.broadcasted_iota(jnp.int32, (rows, tokens), 1)
    rank = lax.broadcasted_iota(jnp.int32, (rows, tokens), 0) & (SLOTS_R - 1)
    low = jnp.zeros((rows, tokens), jnp.int32)
    high = jnp.zeros((rows, tokens), jnp.int32)
    for k in range(MAX_IN_GROUP):
        low = jnp.where(rank == k, first[k], low)
        high = jnp.where(rank == k, end[k], high)
    allowed = (slot >= low) & (slot < high)
    lane = lax.broadcasted_iota(jnp.int32, (rows, HD), 1)
    scale = 1.0 / math.sqrt(HD)
    for t in range(n):
        query_ref[t] = queries[t][...].astype(F32)

    def head(j, carry):
        t = j // kv_per
        i = j - t * kv_per
        shard = lax.rem(facts[1] - t + n, n)
        kv = shard * kv_per + i
        keys = cache_ref[pl.ds(pl.multiple_of(kv * HD, HD), HD), :]
        row, lanes = value_place(kv, tokens)
        values = cache_ref[pl.ds(kv_width + row, tokens), pl.ds(lanes, HD)]
        width = Q_PER_KV * HD
        query = query_ref[t, :, pl.ds(pl.multiple_of(i * width, width), width)]
        scores = dot(by_head(query, 1).astype(BF16), keys) * scale
        scores = jnp.where(allowed, scores, NEGATIVE)
        top = jnp.max(scores, axis=1, keepdims=True)
        weights = jnp.where(allowed, jnp.exp(scores - top), 0.0)
        total = jnp.sum(weights, axis=1, keepdims=True)
        some = total > 0.0
        mixed = dot(weights.astype(BF16), values) / jnp.where(some, total, 1.0)
        level = jnp.where(some, top + jnp.log(jnp.where(some, total, 1.0)), NEGATIVE)
        out_ref[t, pl.ds(pl.multiple_of(i * rows, rows), rows), :] = jnp.concatenate(
            [mixed.astype(BF16), spread(level, lane)], axis=1
        )
        return carry

    lax.fori_loop(0, n * kv_per, head, 0)
    for t in range(n):
        outs[t][...] = out_ref[t]


def combine_kernel(n, count, *refs):
    parts, own_ref, out_ref = refs[:n], refs[n], refs[n + 1]
    own_value = own_ref[:, :HD]
    own_score = own_ref[:, HD : HD + 1]
    mixes = []
    levels = []
    top = own_score
    for t in range(n):
        part = parts[t][...].astype(F32)
        stats = part[:, HD:]
        level = stats[:, 0:1] + stats[:, 32:33] + stats[:, 64:65]
        mixes.append(part[:, :HD])
        levels.append(level)
        top = jnp.maximum(top, level)
    own_weight = jnp.exp(own_score - top)
    total = own_weight
    mixed = own_weight.astype(BF16).astype(F32) * own_value
    for t in range(n):
        weight = jnp.exp(levels[t] - top)
        total = total + weight
        mixed = mixed + weight * mixes[t]
    result = mixed / total
    for h in range(out_ref.shape[2] // HD):
        head = result[h * SLOTS_R : (h + 1) * SLOTS_R].astype(BF16)
        for g in range(count):
            out_ref[g, :, h * HD : (h + 1) * HD] = head


def start_all(pairs, sems):
    copies = [
        pltpu.make_async_copy(source, target, sems.at[i]) for i, (source, target) in enumerate(pairs)
    ]
    for copy in copies:
        copy.start()
    return copies


def project_kernel(count, pick_ref, parts_ref, weight_ref, out_ref, buffer_ref, att_ref, sems):
    steps, _, depth = att_ref.shape

    def copy(j):
        rows = pl.ds(pl.multiple_of(j * depth, depth), depth)
        return pltpu.make_async_copy(weight_ref.at[rows], buffer_ref.at[j], sems.at[j])

    for j in range(steps):
        copy(j).start()
    stacked = jnp.concatenate([parts_ref[g].astype(F32) for g in range(count)], axis=0)
    att = dot(pick_ref[...], stacked.astype(BF16)).astype(BF16)
    for j in range(steps):
        att_ref[j] = att[:, j * depth : (j + 1) * depth]

    def block(j, total):
        copy(j).wait()
        return total + dot(att_ref[j], buffer_ref[j])

    total = lax.fori_loop(0, steps, block, jnp.zeros(out_ref.shape, F32))
    out_ref[...] = total.astype(out_ref.dtype)


def gate_up_kernel(n, count, *refs):
    parts = refs[:n]
    hidden_ref, gain_ref, gate_ref, up_ref, resid_ref, send_ref, gates_ref, ups_ref, sems = refs[n:]
    width = gate_ref.shape[1] // count
    blocks = [pl.ds(g * width, width) for g in range(count)]
    pairs = []
    for b in blocks:
        pairs.append((gate_ref.at[:, b], gates_ref.at[:, b]))
        pairs.append((up_ref.at[:, b], ups_ref.at[:, b]))
    copies = start_all(pairs, sems)
    resid = parts[0][...].astype(F32)
    for part in parts[1:]:
        resid = resid + part[...].astype(F32)
    resid = resid + hidden_ref[...].astype(F32)
    resid_ref[...] = resid
    scaled = (resid * gain_ref[...].astype(F32)).astype(BF16)
    squares = jnp.sum(resid * resid, axis=1, keepdims=True)
    rows = resid.shape[0]
    hi, mid, low = split3(jnp.broadcast_to(squares, (rows, HD)))
    lane = lax.broadcasted_iota(jnp.int32, (rows, HD), 1)
    stats = jnp.where(
        lane < 32, hi.astype(F32), jnp.where(lane < 64, mid.astype(F32), low.astype(F32))
    ).astype(BF16)
    for g in range(count):
        send_ref[g, :, 2 * width :] = stats
    for g in range(count):
        copies[2 * g].wait()
        send_ref[g, :, :width] = dot(scaled, gates_ref[:, blocks[g]]).astype(BF16)
        copies[2 * g + 1].wait()
        send_ref[g, :, width : 2 * width] = dot(scaled, ups_ref[:, blocks[g]]).astype(BF16)


def hidden_kernel(count, features, parts_ref, out_ref):
    width = out_ref.shape[2]
    total = parts_ref[0].astype(F32)
    for g in range(1, count):
        total = total + parts_ref[g].astype(F32)
    stats = total[:, 2 * width :]
    squares = stats[:, 0:1] + stats[:, 32:33] + stats[:, 64:65]
    inverse = lax.rsqrt(squares / features + 1e-05)
    gate = total[:, :width] * inverse
    upper = total[:, width : 2 * width] * inverse
    hidden = (gate / (1.0 + jnp.exp(-gate)) * upper).astype(BF16)
    for g in range(count):
        out_ref[g] = hidden


def down_kernel(count, n, facts, parts_ref, weight_ref, *refs):
    sends, buffer_ref, sems = refs[:n], refs[n], refs[n + 1]
    depth = buffer_ref.shape[1]
    width = sends[0].shape[1]

    def copy(g):
        rows = pl.ds(pl.multiple_of(g * depth, depth), depth)
        return pltpu.make_async_copy(weight_ref.at[rows], buffer_ref.at[g], sems.at[g])

    for g in range(count):
        copy(g).start()

    def block(g, total):
        copy(g).wait()
        return total + dot(parts_ref[g], buffer_ref[g])

    shape = (sends[0].shape[0], weight_ref.shape[1])
    total = lax.fori_loop(0, count, block, jnp.zeros(shape, F32))
    for own in range(n):

        @pl.when(facts[1] == own)
        def _():
            for t in range(n):
                target = (own + t) % n
                sends[t][...] = total[:, target * width : (target + 1) * width]


def row_facts(facts, tokens):
    _, first, end = plan(facts)
    return facts[1] * tokens, facts[facts.shape[0] - 1], first, end


def live_rows(row_first, first, end, tokens):
    row = row_first + lax.broadcasted_iota(jnp.int32, (tokens, HD), 0)
    live = row < 0
    for k in range(MAX_IN_GROUP):
        live = live | ((row >= first[k]) & (row < end[k]))
    return live


def store_bias(bias_ref, row_first, first, end, pieces):
    tokens = bias_ref.shape[0]
    row = row_first + lax.broadcasted_iota(jnp.int32, (tokens, tokens), 0)
    column = lax.broadcasted_iota(jnp.int32, (tokens, tokens), 1)
    low = jnp.full((tokens, tokens), 1 << 30, jnp.int32)
    for k in range(MAX_IN_GROUP):
        low = jnp.where((row >= first[k]) & (row < end[k]), first[k], low)
    for place, t in enumerate(pieces):
        slot = row_first - t * tokens + column
        bias_ref[:, place * tokens : (place + 1) * tokens] = jnp.where(
            (slot >= low) & (slot <= row), 0.0, NEGATIVE
        )


EXP2 = LOG2E / math.sqrt(HD)


def inverse_of(x):
    guess = pl.reciprocal(x, approx=True)
    return guess * (2.0 - x * guess)


DEPTH = 30
CUBIC = (0.99992498, 0.69583478, 0.22606662, 0.07802355)


def power_of_two(x):
    y = x + float(DEPTH)
    whole = y.astype(jnp.int32)
    rest = y - whole.astype(F32)
    value = CUBIC[3] * 2.0**-DEPTH
    for factor in reversed(CUBIC[:3]):
        value = value * rest + factor * 2.0**-DEPTH
    value = value * jnp.left_shift(jnp.ones_like(whole), whole).astype(F32)
    return jnp.where(y < 0.0, 0.0, value)


def by_products(count, t, half, odd):
    if t == 1:
        return True
    if count == 2:
        return False
    if count == 3:
        return t == 2 and half == 0 and odd
    return t % 2 == 0 and t > 0 and half == 0


def interleave(*tasks):
    order = sorted(
        ((k + 0.5) / len(task), which, step)
        for which, task in enumerate(tasks)
        for k, step in enumerate(range(len(task)))
    )
    for _, which, step in order:
        tasks[which][step]()


def prefill_kernel(n, facts, *refs):
    query_hbm, pieces, out_hbm = refs[0], refs[1 : 1 + n], refs[1 + n]
    query_ref, key_ref, value_ref, wide_ref, bias_ref, out_ref = refs[2 + n : 8 + n]
    scores, weights, (query_sems, piece_sems, out_sems) = (
        refs[8 + n : 10 + n],
        refs[10 + n : 12 + n],
        refs[12 + n :],
    )
    tokens = query_ref.shape[1]
    kv_heads = query_ref.shape[0]
    kv_width = key_ref.shape[1]
    row_first, needed, first, end = row_facts(facts, tokens)

    def columns(kv):
        width = Q_PER_KV * HD
        return pl.ds(pl.multiple_of(kv * width, width), width)

    def query_copy(kv):
        return pltpu.make_async_copy(
            query_hbm.at[:, columns(kv)], query_ref.at[kv], query_sems.at[kv]
        )

    def out_copy(kv):
        return pltpu.make_async_copy(out_ref.at[kv], out_hbm.at[:, columns(kv)], out_sems.at[kv])

    @pl.when(needed == 0)
    def _():
        out_ref[...] = jnp.zeros_like(out_ref)
        for kv in range(kv_heads):
            out_copy(kv).start()
        for kv in range(kv_heads):
            out_copy(kv).wait()

    def run(count, lone):
        slots = count * tokens
        chunk = 64
        copies = []
        for t in range(count):
            for part, target in enumerate((key_ref, value_ref)):
                source = pieces[t].at[pl.ds(part * kv_width, kv_width)]
                copies.append(
                    pltpu.make_async_copy(source, target.at[t], piece_sems.at[part, t])
                )
        for copy in copies:
            copy.start()
        for kv in range(kv_heads):
            query_copy(kv).start()
        store_bias(bias_ref, row_first, first, end, range(count))
        live = None if lone else live_rows(row_first, first, end, tokens)
        for copy in copies:
            copy.wait()

        def widen(kv, carry):
            row, lanes = value_place(kv, tokens)
            for t in range(count):
                rows = slice(t * tokens, (t + 1) * tokens)
                wide_ref[kv, rows, :HD] = value_ref[t, pl.ds(row, tokens), pl.ds(lanes, HD)]
                wide_ref[kv, rows, HD:] = jnp.ones((tokens, HD), BF16)
            return carry

        lax.fori_loop(0, kv_heads, widen, 0)

        def place(h):
            kv = h // Q_PER_KV
            return kv, pl.ds(pl.multiple_of((h - kv * Q_PER_KV) * HD, HD), HD)

        def score_steps(h, slot):
            kv, lanes = place(h)
            features = pl.ds(pl.multiple_of(kv * HD, HD), HD)

            def step(t):
                scores[slot][:, t * tokens : (t + 1) * tokens] = dot(
                    query_ref[kv, :, lanes], key_ref[t, features, :]
                )

            return [functools.partial(step, t) for t in range(count)]

        def weight_steps(slot):
            tops = {}

            half = tokens // 2

            def blocks(at):
                for t in range(count):
                    for side in range(2):
                        if t > 0 or side == 0 or at + chunk > half:
                            yield t, side

            def part(at, t, side):
                rows = slice(at, at + chunk)
                lanes = slice(t * tokens + side * half, t * tokens + (side + 1) * half)
                score = scores[slot][rows, lanes]
                return score if lone and t > 0 else score + bias_ref[rows, lanes]

            def top_step(at):
                most = None
                for t, side in blocks(at):
                    block = part(at, t, side)
                    most = block if most is None else jnp.maximum(most, block)
                tops[at] = jnp.max(most, axis=1, keepdims=True)

            def weight_step(at):
                top = tops.pop(at)
                for t, side in blocks(at):
                    power = (part(at, t, side) - top) * EXP2
                    if by_products(count, t, side, at // chunk % 2 == 1):
                        weight = power_of_two(power)
                    else:
                        weight = jnp.exp2(power)
                    lanes = slice(t * tokens + side * half, t * tokens + (side + 1) * half)
                    weights[slot][at : at + chunk, lanes] = weight.astype(BF16)

            starts = list(range(0, tokens, chunk))
            steps = [functools.partial(top_step, at) for at in starts[:2]]
            for i, at in enumerate(starts):
                steps.append(functools.partial(weight_step, at))
                if i + 2 < len(starts):
                    steps.append(functools.partial(top_step, starts[i + 2]))
            return steps

        def value_steps(h, slot):
            kv, lanes = place(h)

            def step(at):
                rows = slice(at, at + tokens // 2)
                mixed = dot(weights[slot][rows, :slots], wide_ref[kv, :slots])
                result = mixed[:, :HD] * inverse_of(mixed[:, HD:])
                if not lone:
                    result = jnp.where(live[rows], result, 0.0)
                out_ref[kv, rows, lanes] = result.astype(BF16)

            return [functools.partial(step, at) for at in range(0, tokens, tokens // 2)]

        for slot in range(2):
            weights[slot][: tokens // 2, tokens // 2 : tokens] = jnp.zeros(
                (tokens // 2, tokens // 2), BF16
            )
        last = kv_heads * Q_PER_KV - 1
        query_copy(0).wait()
        interleave(score_steps(jnp.int32(0), 0))
        interleave(score_steps(jnp.int32(1), 1), weight_steps(0))

        def kv_step(kv, carry):
            @pl.when(kv + 1 < kv_heads)
            def _():
                query_copy(kv + 1).wait()

            def two_heads(j, inner):
                for slot in range(2):
                    h = kv * Q_PER_KV + 2 * j + slot
                    interleave(
                        score_steps(jnp.minimum(h + 2, last), slot),
                        weight_steps(1 - slot),
                        value_steps(h, slot),
                    )
                return inner

            lax.fori_loop(0, Q_PER_KV // 2, two_heads, 0)
            out_copy(kv).start()
            return carry

        lax.fori_loop(0, kv_heads, kv_step, 0)
        for kv in range(kv_heads):
            out_copy(kv).wait()

    lone = needed < 0
    for k in range(MAX_IN_GROUP):
        lone = lone | (
            (first[k] <= row_first - (needed - 1) * tokens) & (end[k] >= row_first + tokens)
        )
    before = 0
    for count in sorted({c for c in (1, 2, 3, n) if c <= n}):
        here = (needed > before) & (needed <= count)
        exact = (needed == count) & lone
        before = count

        @pl.when(exact)
        def _():
            run(count, True)

        @pl.when(here & jnp.logical_not(exact))
        def _():
            run(count, False)


def call(body, scalars, args, outs, *, grid=None, in_specs=None, out_specs=None, scratch=(), cost, vmem=6, aliases=None):
    whole = pl.BlockSpec(memory_space=pltpu.VMEM)
    if grid is None:
        grid = (1,)
    flops, exps = cost
    moved = sum(a.size * a.dtype.itemsize for a in args) + sum(
        o.size * o.dtype.itemsize for o in outs
    )
    return pl.pallas_call(
        body,
        out_shape=list(outs),
        grid_spec=pltpu.PrefetchScalarGridSpec(
            num_scalar_prefetch=len(scalars),
            grid=grid,
            in_specs=in_specs or [whole] * len(args),
            out_specs=out_specs or [whole] * len(outs),
            scratch_shapes=list(scratch),
        ),
        compiler_params=pltpu.CompilerParams(
            dimension_semantics=("arbitrary",) * len(grid), vmem_limit_bytes=int(vmem * MIB)
        ),
        input_output_aliases=aliases or {},
        cost_estimate=pl.CostEstimate(flops=flops, bytes_accessed=moved, transcendentals=exps),
    )(*scalars, *args)


def shift(x, axis, count, t):
    return lax.ppermute(x, axis, [(i, (i + t) % count) for i in range(count)])


def shards(
    lengths,
    group_of,
    query_pre,
    key_pre,
    value_pre,
    query_new,
    key_new,
    value_new,
    hidden_new,
    out_weight,
    norm_gain,
    gate_weight,
    up_weight,
    down_weight,
):
    n = lax.axis_size("seq")
    count = lax.axis_size("grp")
    seq = lax.axis_index("seq").astype(jnp.int32)
    group = lax.axis_index("grp").astype(jnp.int32)
    tokens = query_pre.shape[0]
    reqs = query_new.shape[0]
    kv_heads = key_pre.shape[1] // HD
    shard_width = query_new.shape[1]
    shard_heads = shard_width // HD
    columns = out_weight.shape[1]
    shape = jax.ShapeDtypeStruct
    vmem = pl.BlockSpec(memory_space=pltpu.VMEM)
    anywhere = pl.BlockSpec(memory_space=pl.ANY)
    dma = pltpu.SemaphoreType.DMA
    facts = jnp.concatenate([jnp.stack([group, seq]), group_of, lengths])
    scalars = (facts,)

    def to_seq(x):
        return [x] + [shift(x, "seq", n, t) for t in range(1, n)]

    def to_grp(x):
        return lax.all_to_all(x, "grp", split_axis=0, concat_axis=0, tiled=True)

    def tie(x, after):
        return lax.optimization_barrier((x, after))[0]

    def up(x, step, after):
        return lax.ppermute(tie(x, after), "seq", [(i, i + 1) for i in range(step - 1, n - 1)])

    pieces = call(
        pack_kernel,
        (),
        (key_pre, value_pre),
        (shape((2 * kv_heads * HD, tokens), BF16),),
        cost=(key_pre.size, 0),
    )
    pieces = list(pieces)

    query, own = call(
        select_kernel,
        scalars,
        (jnp.concatenate([query_new, key_new, value_new], axis=1),),
        (shape((SLOTS_R, shard_width), BF16), shape((shard_heads * SLOTS_R, 2 * HD), F32)),
        cost=(2 * 8 * reqs * shard_width, 0),
    )
    queries = to_seq(query)
    rows = shard_heads * SLOTS_R
    partials = call(
        functools.partial(partial_kernel, n),
        scalars,
        (*queries, pieces[0]),
        [shape((rows, 2 * HD), BF16)] * n,
        scratch=(
            pltpu.VMEM((n, SLOTS_R, shard_width), F32),
            pltpu.VMEM((n, rows, 2 * HD), BF16),
        ),
        cost=(4 * n * rows * tokens * HD, n * rows * tokens),
    )
    partials = [partials[0]] + [shift(partials[t], "seq", n, n - t) for t in range(1, n)]
    pieces.append(up(pieces[-1], 1, partials[1:]))
    (att,) = call(
        functools.partial(combine_kernel, n, count),
        (),
        (*partials, own),
        (shape((count, SLOTS_R, shard_width), BF16),),
        cost=(8 * n * rows * HD, n * rows),
    )
    atts = to_grp(att)

    index = jnp.arange(reqs, dtype=jnp.int32)
    groups = tie(group_of, att)
    same = groups[None, :] == groups[:, None]
    rank = jnp.sum(jnp.where(same & (index[None, :] < index[:, None]), 1, 0), axis=1)
    place = groups * SLOTS_R + rank
    pick = (place[:, None] == jnp.arange(count * SLOTS_R, dtype=jnp.int32)[None, :]).astype(BF16)
    steps = 8
    depth = shard_width // steps
    (proj,) = call(
        functools.partial(project_kernel, count),
        (),
        (pick, atts, out_weight),
        (shape((reqs, columns), BF16),),
        in_specs=[vmem, vmem, anywhere],
        scratch=(
            pltpu.VMEM((steps, depth, columns), BF16),
            pltpu.VMEM((steps, reqs, depth), BF16),
            dma((steps,)),
        ),
        cost=(2 * reqs * shard_width * columns, 0),
        vmem=STREAM + 3,
    )
    projs = to_seq(proj)
    if n > 2:
        pieces.append(up(pieces[-1], 2, projs[1:]))

    hidden_shard = gate_weight.shape[1]
    width = hidden_shard // count
    resid, terms = call(
        functools.partial(gate_up_kernel, n, count),
        (),
        (*projs, hidden_new, norm_gain.reshape(1, -1), gate_weight, up_weight),
        [shape((reqs, columns), F32), shape((count, reqs, 2 * width + HD), BF16)],
        in_specs=[vmem] * (n + 2) + [anywhere] * 2,
        scratch=(
            pltpu.VMEM(gate_weight.shape, BF16),
            pltpu.VMEM(up_weight.shape, BF16),
            dma((2 * count,)),
        ),
        cost=(4 * reqs * columns * hidden_shard, 0),
        vmem=STREAM,
    )
    terms = to_grp(terms)
    (hidden,) = call(
        functools.partial(hidden_kernel, count, columns * count),
        (),
        (terms,),
        (shape((count, reqs, width), BF16),),
        cost=(8 * count * reqs * width, reqs * width),
    )
    if n > 3:
        pieces.append(up(pieces[-1], 3, hidden))
    hiddens = to_grp(hidden)
    share = columns // n
    downs = call(
        functools.partial(down_kernel, count, n),
        scalars,
        (hiddens, down_weight),
        [shape((reqs, share), F32)] * n,
        in_specs=[vmem, anywhere],
        scratch=(pltpu.VMEM((count, width, columns), BF16), dma((count,))),
        cost=(2 * reqs * columns * hidden_shard, 0),
        vmem=STREAM,
    )
    total = lax.dynamic_slice_in_dim(resid, seq * share, share, 1) + downs[0]
    arrived = [shift(downs[t], "seq", n, t) for t in range(1, n)]
    for part in arrived:
        total = total + part
    decode_hidden = total.astype(BF16)
    for step in range(len(pieces), n):
        pieces.append(up(pieces[-1], step, pieces[-1]))

    first = jnp.sum(jnp.where(same & (index[None, :] < index[:, None]), lengths[None, :], 0), axis=1)
    row_first = seq * tokens
    meets = (group_of == group) & (first + lengths > row_first) & (first < row_first + tokens)
    lowest = jnp.min(jnp.where(meets, first, row_first + tokens))
    scalars = (jnp.concatenate([facts, (seq - lax.div(lowest, tokens) + 1)[None]]),)
    wide = Q_PER_KV * HD
    (prefill,) = call(
        functools.partial(prefill_kernel, n),
        scalars,
        (query_pre, *pieces),
        (shape(query_pre.shape, BF16),),
        in_specs=[anywhere] * (1 + n),
        out_specs=[anywhere],
        scratch=[
            pltpu.VMEM((kv_heads, tokens, wide), BF16),
            pltpu.VMEM((n, kv_heads * HD, tokens), BF16),
            pltpu.VMEM((n, kv_heads * HD, tokens), BF16),
            pltpu.VMEM((kv_heads, n * tokens, 2 * HD), BF16),
            pltpu.VMEM((tokens, n * tokens), F32),
            pltpu.VMEM((kv_heads, tokens, wide), BF16),
        ]
        + [pltpu.VMEM((tokens, n * tokens), F32)] * 2
        + [pltpu.VMEM((tokens, n * tokens), BF16)] * 2
        + [dma((kv_heads,)), dma((2, n)), dma((kv_heads,))],
        cost=(8 * n * tokens * query_pre.size, n * tokens * query_pre.size // HD),
        vmem=STREAM + 3,
    )
    return (prefill, decode_hidden)


def solution(mesh):
    return jax.shard_map(
        shards,
        mesh=mesh,
        in_specs=(
            P(),
            P(),
            P(("grp", "seq"), None),
            P(("grp", "seq"), None),
            P(("grp", "seq"), None),
            P(None, "seq"),
            P(None, "seq"),
            P(None, "seq"),
            P(None, "grp"),
            P("seq", "grp"),
            P("grp"),
            P("grp", "seq"),
            P("grp", "seq"),
            P("seq", "grp"),
        ),
        out_specs=(P(("grp", "seq"), None), P(None, ("grp", "seq"))),
        check_vma=False,
    )
```

profile of v0, /device:TPU:27, one launch (start us, length us, event | category | flops | bytes accessed | tf_op | source)
XLA Modules:
  0.0 145.2 jit_solution(4462047551946564130)
XLA Ops:
  0.6 0.9 pad_maximum_fusion.new_ref
  1.5 0.7 pad_add_fusion.facts
  2.3 0.8 shard_map.149
  3.1 0.2 collective-permute-start.2
  3.3 0.1 collective-permute-start.1
  3.3 3.0 %collective-permute-start = (bf16[4,2048]{1,0:T(4,128)(2,1)S(1)}, bf16[4,2048]{1,0:T(4,128)(2,1)S(1)}, u32[]{:S(2)}, u32[]{:S(2)}) collective-permute-start(bf16[4,2048]{1,0:T(4,128)(2,1)S(1)} %get-tuple-element.18.refs_0_), channel_id=1, source_target_pairs={{0,1},{1,2},{2,3},{3,0},{4,5},{5,6},{6,7},{7,4},{8,9},{9,10},{10,1... | collective-permute-start | bytes 49160 | tf_op jit(solution)/shard_map/ppermute | solution.py:577
  6.4 1.0 copy-done.1
  7.4 1.0 copy-done.2
  8.5 0.2 shard_map.150.refs_4_.refs_1_
  8.7 3.4 %shard_map.151 = (bf16[64,256]{1,0:T(8,128)(2,1)S(1)}, bf16[64,256]{1,0:T(8,128)(2,1)S(1)}, bf16[64,256]{1,0:T(8,128)(2,1)S(1)}, bf16[64,256]{1,0:T(8,128)(2,1)S(1)}) custom-call(s32[34]{0:T(128)S(1)} %pad_add_fusion.facts, bf16[4,2048]{1,0:T(4,128)(2,1)S(1)} %get-tuple-element.18.refs_0_, bf16[4,2048]{1,0:T(4,128)(2,1)S(1)} %collective-permute-done.refs_1_, ...), custom_call_target="tpu_custom_call" | custom-call | flops 33554432 | bytes 1245184 | tf_op jit(solution)/shard_map/pallas_call | solution.py:558
  12.1 0.7 collective-permute-start.3
  12.9 1.7 %collective-permute-start.4 = (bf16[64,256]{1,0:T(8,128)(2,1)S(1)}, bf16[64,256]{1,0:T(8,128)(2,1)S(1)}, u32[]{:S(2)}, u32[]{:S(2)}) collective-permute-start(bf16[64,256]{1,0:T(8,128)(2,1)S(1)} %get-tuple-element.21), channel_id=1, source_target_pairs={{0,2},{1,3},{2,0},{3,1},{4,6},{5,7},{6,4},{7,5},{8,10},{9,11},{10,... | collective-permute-start | bytes 98312 | tf_op jit(solution)/shard_map/ppermute | solution.py:577
  14.5 1.5 %collective-permute-start.5 = (bf16[64,256]{1,0:T(8,128)(2,1)S(1)}, bf16[64,256]{1,0:T(8,128)(2,1)S(1)}, u32[]{:S(2)}, u32[]{:S(2)}) collective-permute-start(bf16[64,256]{1,0:T(8,128)(2,1)S(1)} %get-tuple-element.22), channel_id=1, source_target_pairs={{0,1},{1,2},{2,3},{3,0},{4,5},{5,6},{6,7},{7,4},{8,9},{9,10},{10,1... | collective-permute-start | bytes 98312 | tf_op jit(solution)/shard_map/ppermute | solution.py:577
  16.0 0.8 collective-permute-done.3.refs_1_
  16.9 0.4 collective-permute-done.5.refs_3_
  17.3 1.3 collective-permute-start.6
  18.6 0.9 shard_map.152
  19.5 7.7 %all-to-all-start = ((bf16[8,4,2048]{2,1,0:T(4,128)(2,1)}), bf16[8,4,2048]{2,1,0:T(4,128)(2,1)S(1)}, u32[]{:S(2)}, u32[]{:S(2)}) async-start(bf16[8,4,2048]{2,1,0:T(4,128)(2,1)} %shard_map.152), calls=%async_computation | async-start | bytes 262144 | tf_op jit(solution)/shard_map/all_to_all | solution.py:617
  27.2 0.9 select_reduce_fusion
  28.1 0.7 multiply_add_fusion
  28.8 0.7 fusion.1.pick_ref
  29.5 1.4 all-to-all-done.parts_ref
  30.9 0.7 copy-done.5
  31.6 4.1 %shard_map.153.refs_0_ = bf16[16,1024]{1,0:T(8,128)(2,1)} custom-call(bf16[16,32]{1,0:T(8,128)(2,1)} %fusion.1.pick_ref, bf16[8,4,2048]{2,1,0:T(4,128)(2,1)} %copy-done.5, bf16[2048,1024]{1,0:T(8,128)(2,1)} %weight_ref.2), custom_call_target="tpu_custom_call" | custom-call | flops 67108864 | bytes 4359168 | tf_op jit(solution)/shard_map/pallas_call | solution.py:558
  35.7 2.4 %collective-permute-start.9 = (bf16[16,1024]{1,0:T(8,128)(2,1)}, bf16[16,1024]{1,0:T(8,128)(2,1)S(1)}, u32[]{:S(2)}, u32[]{:S(2)}) collective-permute-start(bf16[16,1024]{1,0:T(8,128)(2,1)} %shard_map.153.refs_0_), channel_id=1, source_target_pairs={{0,3},{1,0},{2,1},{3,2},{4,7},{5,4},{6,5},{7,6},{8,11},{9,8},{10,9... | collective-permute-start | bytes 98312 | tf_op jit(solution)/shard_map/ppermute | solution.py:577
  38.1 0.9 collective-permute-start.8
  39.0 1.5 %collective-permute-start.7 = (bf16[16,1024]{1,0:T(8,128)(2,1)}, bf16[16,1024]{1,0:T(8,128)(2,1)S(1)}, u32[]{:S(2)}, u32[]{:S(2)}) collective-permute-start(bf16[16,1024]{1,0:T(8,128)(2,1)} %shard_map.153.refs_0_), channel_id=1, source_target_pairs={{0,1},{1,2},{2,3},{3,0},{4,5},{5,6},{6,7},{7,4},{8,9},{9,10},{10,1... | collective-permute-start | bytes 98312 | tf_op jit(solution)/shard_map/ppermute | solution.py:577
  40.5 1.8 %collective-permute-done.9.refs_3_ = bf16[16,1024]{1,0:T(8,128)(2,1)S(1)} collective-permute-done((bf16[16,1024]{1,0:T(8,128)(2,1)}, bf16[16,1024]{1,0:T(8,128)(2,1)S(1)}, u32[]{:S(2)}, u32[]{:S(2)}) %collective-permute-start.9) | collective-permute-done | bytes 32800 | tf_op jit(solution)/shard_map/ppermute | solution.py:577
  42.3 1.3 collective-permute-done.8.refs_2_
  43.7 1.3 collective-permute-start.10
  45.0 0.6 reshape.11.refs_5_
  45.6 7.8 %shard_map.154 = (f32[16,1024]{1,0:T(8,128)}, bf16[8,16,1152]{2,1,0:T(8,128)(2,1)}) custom-call(bf16[16,1024]{1,0:T(8,128)(2,1)} %shard_map.153.refs_0_, bf16[16,1024]{1,0:T(8,128)(2,1)} %copy-done.8, bf16[16,1024]{1,0:T(8,128)(2,1)} %copy-done.7, bf16[16,1024]{1,0:T(8,128)(2,1)} %copy-done.6, bf16[16,1024]{1,0:T(8,128)(2,1)} %refs_4_.1, ...), custom_call_target="tpu_custom_call" | custom-call | flops 268435456 | bytes 17303552 | tf_op jit(solution)/shard_map/pallas_call | solution.py:558
  53.5 14.5 %all_to_all.15.parts_ref = bf16[8,16,1152]{2,1,0:T(8,128)(2,1)S(1)} all-to-all(bf16[8,16,1152]{2,1,0:T(8,128)(2,1)} %get-tuple-element.27), channel_id=1, replica_groups=mesh['grp'=8,'seq'=4] {'grp'}, dimensions={0} | all-to-all | bytes 589824 | tf_op jit(solution)/shard_map/all_to_all | solution.py:617
  68.0 0.8 shard_map.155
  68.8 1.3 collective-permute-start.11
  70.1 6.2 %all-to-all-start.2 = ((bf16[8,16,512]{2,1,0:T(8,128)(2,1)}), bf16[8,16,512]{2,1,0:T(8,128)(2,1)S(1)}, u32[]{:S(2)}, u32[]{:S(2)}) async-start(bf16[8,16,512]{2,1,0:T(8,128)(2,1)} %shard_map.155), calls=%async_computation.2 | async-start | bytes 262144 | tf_op jit(solution)/shard_map/all_to_all | solution.py:617
  76.3 3.7 %all-to-all-done.2.parts_ref = bf16[8,16,512]{2,1,0:T(8,128)(2,1)S(1)} async-done(((bf16[8,16,512]{2,1,0:T(8,128)(2,1)}), bf16[8,16,512]{2,1,0:T(8,128)(2,1)S(1)}, u32[]{:S(2)}, u32[]{:S(2)}) %all-to-all-start.2) | async-done | bytes 131104 | tf_op jit(solution)/shard_map/all_to_all | solution.py:617
  80.0 0.7 copy-done.4
  80.7 5.9 %shard_map.157 = (f32[16,256]{1,0:T(8,128)}, f32[16,256]{1,0:T(8,128)}, f32[16,256]{1,0:T(8,128)}, f32[16,256]{1,0:T(8,128)}) custom-call(s32[34]{0:T(128)} %copy-done.3, bf16[8,16,512]{2,1,0:T(8,128)(2,1)} %copy-done.4, bf16[4096,1024]{1,0:T(8,128)(2,1)} %weight_ref.3), custom_call_target="tpu_custom_call" | custom-call | flops 134217728 | bytes 8585216 | tf_op jit(solution)/shard_map/pallas_call | solution.py:558
  86.6 0.1 collective-permute-start.12
  86.7 3.6 %collective-permute-start.13 = (f32[16,256]{1,0:T(8,128)}, f32[16,256]{1,0:T(8,128)S(1)}, u32[]{:S(2)}, u32[]{:S(2)}) collective-permute-start(f32[16,256]{1,0:T(8,128)} %get-tuple-element.32), channel_id=1, source_target_pairs={{0,2},{1,3},{2,0},{3,1},{4,6},{5,7},{6,4},{7,5},{8,10},{9,11},{10,... | collective-permute-start | bytes 49160 | tf_op jit(solution)/shard_map/ppermute | solution.py:577
  90.3 0.6 fusion.2
  92.9 0.6 concatenate.12.facts
  93.4 0.8 collective-permute-done.12
  94.3 0.7 collective-permute-done.14
  95.0 1.3 add_convert_fusion
  96.3 1.0 copy-done.14
  97.3 47.8 %shard_map.156 = bf16[256,8192]{1,0:T(8,128)(2,1)} custom-call(s32[35]{0:T(128)} %concatenate.12.facts, bf16[256,8192]{1,0:T(8,128)(2,1)} %refs_0_.1, bf16[2048,256]{1,0:T(8,128)(2,1)} %copy-done, bf16[2048,256]{1,0:T(8,128)(2,1)} %copy-done.12, bf16[2048,256]{1,0:T(8,128)(2,1)} %copy-done.13, bf16[2048,256]{1,0:T(8,128)(2,1)} %copy-done.14), custom_call_target="tpu_custom_call" | custom-call | flops 17179869184 | bytes 12582912 | tf_op jit(solution)/shard_map/pallas_call | solution.py:558
  (35 shorter events, 0.1 us)
Async XLA Ops:
  0.6 44.3 %copy-start.11 = (bf16[1024]{0:T(1024)(128)(2,1)S(1)}, bf16[1024]{0:T(1024)(128)(2,1)}, u32[]{:S(2)}) copy-start(bf16[1024]{0:T(1024)(128)(2,1)} %param.24) | copy-start | bytes 6148
  2.3 51.2 %copy-start.3 = (s32[34]{0:T(128)}, s32[34]{0:T(128)S(1)}, u32[]{:S(2)}) copy-start(s32[34]{0:T(128)S(1)} %pad_add_fusion.facts) | copy-start | bytes 412
  3.1 5.6 %collective-permute-start.2 = (bf16[4,2048]{1,0:T(4,128)(2,1)S(1)}, bf16[4,2048]{1,0:T(4,128)(2,1)S(1)}, u32[]{:S(2)}, u32[]{:S(2)}) collective-permute-start(bf16[4,2048]{1,0:T(4,128)(2,1)S(1)} %get-tuple-element.18.refs_0_), channel_id=1, source_target_pairs={{0,3},{1,0},{2,1},{3,2},{4,7},{5,4},{6,5},{7,6},{8,11},{9,8},{10,9... | collective-permute-start | bytes 49160 | tf_op jit(solution)/shard_map/ppermute | solution.py:577
  3.3 5.4 %collective-permute-start.1 = (bf16[4,2048]{1,0:T(4,128)(2,1)S(1)}, bf16[4,2048]{1,0:T(4,128)(2,1)S(1)}, u32[]{:S(2)}, u32[]{:S(2)}) collective-permute-start(bf16[4,2048]{1,0:T(4,128)(2,1)S(1)} %get-tuple-element.18.refs_0_), channel_id=1, source_target_pairs={{0,2},{1,3},{2,0},{3,1},{4,6},{5,7},{6,4},{7,5},{8,10},{9,11},{10,... | collective-permute-start | bytes 49160 | tf_op jit(solution)/shard_map/ppermute | solution.py:577
  3.3 5.4 %collective-permute-start = (bf16[4,2048]{1,0:T(4,128)(2,1)S(1)}, bf16[4,2048]{1,0:T(4,128)(2,1)S(1)}, u32[]{:S(2)}, u32[]{:S(2)}) collective-permute-start(bf16[4,2048]{1,0:T(4,128)(2,1)S(1)} %get-tuple-element.18.refs_0_), channel_id=1, source_target_pairs={{0,1},{1,2},{2,3},{3,0},{4,5},{5,6},{6,7},{7,4},{8,9},{9,10},{10,1... | collective-permute-start | bytes 49160 | tf_op jit(solution)/shard_map/ppermute | solution.py:577
  6.4 1.0 copy-start.1
  7.4 1.0 copy-start.2
  8.7 44.8 %copy-start = (bf16[2048,256]{1,0:T(8,128)(2,1)}, bf16[2048,256]{1,0:T(8,128)(2,1)S(1)}, u32[]{:S(2)}) copy-start(bf16[2048,256]{1,0:T(8,128)(2,1)S(1)} %shard_map.150.refs_4_.refs_1_) | copy-start | bytes 3145732
  12.1 4.7 %collective-permute-start.3 = (bf16[64,256]{1,0:T(8,128)(2,1)S(1)}, bf16[64,256]{1,0:T(8,128)(2,1)S(1)}, u32[]{:S(2)}, u32[]{:S(2)}) collective-permute-start(bf16[64,256]{1,0:T(8,128)(2,1)S(1)} %get-tuple-element.20), channel_id=1, source_target_pairs={{0,3},{1,0},{2,1},{3,2},{4,7},{5,4},{6,5},{7,6},{8,11},{9,8},{10,9... | collective-permute-start | bytes 98312 | tf_op jit(solution)/shard_map/ppermute | solution.py:577
  12.9 4.0 %collective-permute-start.4 = (bf16[64,256]{1,0:T(8,128)(2,1)S(1)}, bf16[64,256]{1,0:T(8,128)(2,1)S(1)}, u32[]{:S(2)}, u32[]{:S(2)}) collective-permute-start(bf16[64,256]{1,0:T(8,128)(2,1)S(1)} %get-tuple-element.21), channel_id=1, source_target_pairs={{0,2},{1,3},{2,0},{3,1},{4,6},{5,7},{6,4},{7,5},{8,10},{9,11},{10,... | collective-permute-start | bytes 98312 | tf_op jit(solution)/shard_map/ppermute | solution.py:577
  14.5 2.8 %collective-permute-start.5 = (bf16[64,256]{1,0:T(8,128)(2,1)S(1)}, bf16[64,256]{1,0:T(8,128)(2,1)S(1)}, u32[]{:S(2)}, u32[]{:S(2)}) collective-permute-start(bf16[64,256]{1,0:T(8,128)(2,1)S(1)} %get-tuple-element.22), channel_id=1, source_target_pairs={{0,1},{1,2},{2,3},{3,0},{4,5},{5,6},{6,7},{7,4},{8,9},{9,10},{10,1... | collective-permute-start | bytes 98312 | tf_op jit(solution)/shard_map/ppermute | solution.py:577
  17.3 26.3 %collective-permute-start.6 = (bf16[2048,256]{1,0:T(8,128)(2,1)S(1)}, bf16[2048,256]{1,0:T(8,128)(2,1)S(1)}, u32[]{:S(2)}, u32[]{:S(2)}) collective-permute-start(bf16[2048,256]{1,0:T(8,128)(2,1)S(1)} %shard_map.150.refs_4_.refs_1_), channel_id=1, source_target_pairs={{0,1},{1,2},{2,3},{4,5},{5,6},{6,7},{8,9},{9,10},{10,11},{12,13},{... | collective-permute-start | bytes 3145736 | tf_op jit(solution)/shard_map/ppermute | solution.py:623
  19.5 11.4 %all-to-all-start = ((bf16[8,4,2048]{2,1,0:T(4,128)(2,1)}), bf16[8,4,2048]{2,1,0:T(4,128)(2,1)S(1)}, u32[]{:S(2)}, u32[]{:S(2)}) async-start(bf16[8,4,2048]{2,1,0:T(4,128)(2,1)} %shard_map.152), calls=%async_computation | async-start | bytes 262144 | tf_op jit(solution)/shard_map/all_to_all | solution.py:617
  30.9 0.7 copy-start.5
  35.7 6.6 %collective-permute-start.9 = (bf16[16,1024]{1,0:T(8,128)(2,1)}, bf16[16,1024]{1,0:T(8,128)(2,1)S(1)}, u32[]{:S(2)}, u32[]{:S(2)}) collective-permute-start(bf16[16,1024]{1,0:T(8,128)(2,1)} %shard_map.153.refs_0_), channel_id=1, source_target_pairs={{0,3},{1,0},{2,1},{3,2},{4,7},{5,4},{6,5},{7,6},{8,11},{9,8},{10,9... | collective-permute-start | bytes 98312 | tf_op jit(solution)/shard_map/ppermute | solution.py:577
  38.1 5.5 %collective-permute-start.8 = (bf16[16,1024]{1,0:T(8,128)(2,1)}, bf16[16,1024]{1,0:T(8,128)(2,1)S(1)}, u32[]{:S(2)}, u32[]{:S(2)}) collective-permute-start(bf16[16,1024]{1,0:T(8,128)(2,1)} %shard_map.153.refs_0_), channel_id=1, source_target_pairs={{0,2},{1,3},{2,0},{3,1},{4,6},{5,7},{6,4},{7,5},{8,10},{9,11},{10,... | collective-permute-start | bytes 98312 | tf_op jit(solution)/shard_map/ppermute | solution.py:577
  39.0 4.6 %collective-permute-start.7 = (bf16[16,1024]{1,0:T(8,128)(2,1)}, bf16[16,1024]{1,0:T(8,128)(2,1)S(1)}, u32[]{:S(2)}, u32[]{:S(2)}) collective-permute-start(bf16[16,1024]{1,0:T(8,128)(2,1)} %shard_map.153.refs_0_), channel_id=1, source_target_pairs={{0,1},{1,2},{2,3},{3,0},{4,5},{5,6},{6,7},{7,4},{8,9},{9,10},{10,1... | collective-permute-start | bytes 98312 | tf_op jit(solution)/shard_map/ppermute | solution.py:577
  42.3 3.3 %copy-start.6 = (bf16[16,1024]{1,0:T(8,128)(2,1)}, bf16[16,1024]{1,0:T(8,128)(2,1)S(1)}, u32[]{:S(2)}) copy-start(bf16[16,1024]{1,0:T(8,128)(2,1)S(1)} %collective-permute-done.9.refs_3_) | copy-start | bytes 98308
  43.6 1.9 %copy-start.7 = (bf16[16,1024]{1,0:T(8,128)(2,1)}, bf16[16,1024]{1,0:T(8,128)(2,1)S(1)}, u32[]{:S(2)}) copy-start(bf16[16,1024]{1,0:T(8,128)(2,1)S(1)} %collective-permute-done.8.refs_2_) | copy-start | bytes 98308
  43.6 1.9 %copy-start.8 = (bf16[16,1024]{1,0:T(8,128)(2,1)}, bf16[16,1024]{1,0:T(8,128)(2,1)S(1)}, u32[]{:S(2)}) copy-start(bf16[16,1024]{1,0:T(8,128)(2,1)S(1)} %collective-permute-done.7.refs_1_) | copy-start | bytes 98308
  43.6 9.8 %copy-start.12 = (bf16[2048,256]{1,0:T(8,128)(2,1)}, bf16[2048,256]{1,0:T(8,128)(2,1)S(1)}, u32[]{:S(2)}) copy-start(bf16[2048,256]{1,0:T(8,128)(2,1)S(1)} %collective-permute-done.6.refs_2_) | copy-start | bytes 3145732
  43.7 25.1 %collective-permute-start.10 = (bf16[2048,256]{1,0:T(8,128)(2,1)S(1)}, bf16[2048,256]{1,0:T(8,128)(2,1)S(1)}, u32[]{:S(2)}, u32[]{:S(2)}) collective-permute-start(bf16[2048,256]{1,0:T(8,128)(2,1)S(1)} %collective-permute-done.6.refs_2_), channel_id=1, source_target_pairs={{1,2},{2,3},{5,6},{6,7},{9,10},{10,11},{13,14},{14,15},{17,18},{18... | collective-permute-start | bytes 3145736 | tf_op jit(solution)/shard_map/ppermute | solution.py:623
  53.5 36.8 %copy-start.9 = (s32[16]{0:T(128)S(1)}, s32[16]{0:T(128)}, u32[]{:S(2)}) copy-start(s32[16]{0:T(128)} %param.15) | copy-start | bytes 196
  53.5 36.8 %copy-start.10 = (s32[16]{0:T(128)S(1)}, s32[16]{0:T(128)}, u32[]{:S(2)}) copy-start(s32[16]{0:T(128)} %param.14) | copy-start | bytes 196
  68.8 27.5 %copy-start.13 = (bf16[2048,256]{1,0:T(8,128)(2,1)}, bf16[2048,256]{1,0:T(8,128)(2,1)S(1)}, u32[]{:S(2)}) copy-start(bf16[2048,256]{1,0:T(8,128)(2,1)S(1)} %collective-permute-done.10.refs_3_) | copy-start | bytes 3145732
  68.8 27.5 %collective-permute-start.11 = (bf16[2048,256]{1,0:T(8,128)(2,1)S(1)}, bf16[2048,256]{1,0:T(8,128)(2,1)S(1)}, u32[]{:S(2)}, u32[]{:S(2)}) collective-permute-start(bf16[2048,256]{1,0:T(8,128)(2,1)S(1)} %collective-permute-done.10.refs_3_), channel_id=1, source_target_pairs={{2,3},{6,7},{10,11},{14,15},{18,19},{22,23},{26,27},{30,31}} | collective-permute-start | bytes 3145736 | tf_op jit(solution)/shard_map/ppermute | solution.py:623
  70.1 9.9 %all-to-all-start.2 = ((bf16[8,16,512]{2,1,0:T(8,128)(2,1)}), bf16[8,16,512]{2,1,0:T(8,128)(2,1)S(1)}, u32[]{:S(2)}, u32[]{:S(2)}) async-start(bf16[8,16,512]{2,1,0:T(8,128)(2,1)} %shard_map.155), calls=%async_computation.2 | async-start | bytes 262144 | tf_op jit(solution)/shard_map/all_to_all | solution.py:617
  80.0 0.7 copy-start.4
  86.6 7.7 %collective-permute-start.12 = (f32[16,256]{1,0:T(8,128)}, f32[16,256]{1,0:T(8,128)S(1)}, u32[]{:S(2)}, u32[]{:S(2)}) collective-permute-start(f32[16,256]{1,0:T(8,128)} %get-tuple-element.31), channel_id=1, source_target_pairs={{0,1},{1,2},{2,3},{3,0},{4,5},{5,6},{6,7},{7,4},{8,9},{9,10},{10,1... | collective-permute-start | bytes 49160 | tf_op jit(solution)/shard_map/ppermute | solution.py:577
  86.7 7.6 %collective-permute-start.13 = (f32[16,256]{1,0:T(8,128)}, f32[16,256]{1,0:T(8,128)S(1)}, u32[]{:S(2)}, u32[]{:S(2)}) collective-permute-start(f32[16,256]{1,0:T(8,128)} %get-tuple-element.32), channel_id=1, source_target_pairs={{0,2},{1,3},{2,0},{3,1},{4,6},{5,7},{6,4},{7,5},{8,10},{9,11},{10,... | collective-permute-start | bytes 49160 | tf_op jit(solution)/shard_map/ppermute | solution.py:577
  90.2 4.7 %collective-permute-start.14 = (f32[16,256]{1,0:T(8,128)}, f32[16,256]{1,0:T(8,128)S(1)}, u32[]{:S(2)}, u32[]{:S(2)}) collective-permute-start(f32[16,256]{1,0:T(8,128)} %get-tuple-element.33), channel_id=1, source_target_pairs={{0,3},{1,0},{2,1},{3,2},{4,7},{5,4},{6,5},{7,6},{8,11},{9,8},{10,9... | collective-permute-start | bytes 49160 | tf_op jit(solution)/shard_map/ppermute | solution.py:577
  96.3 1.0 copy-start.14
where the time goes:
time: 147 us; the launch traced here: 145 us
  Pallas kernels  71.8 us (49%)
  starting transfers between devices  33.5 us (23%)
  blocking collectives  14.5 us (10%)
  waiting for transfers between devices  11 us (7%)
  other arithmetic  5.85 us (4%)
  local copies, waits for them, and re-layouts  5.59 us (4%)
  between operations  2.95 us (2%)
    pallas_call x9, Pallas kernels, call(): pl.pallas_call(body, out_shape=list(outs), grid_spec=pltpu.PrefetchScalar...  71.8 us
    ppermute x12, starting transfers between devices, shift(): return lax.ppermute(x, axis, [(i, (i + t) % count) for i in range(count)])  15.7 us
    all_to_all x1, blocking collectives, to_grp(): return lax.all_to_all(x, 'grp', split_axis=0, concat_axis=0, tiled=True)  14.5 us
    all_to_all x2, starting transfers between devices, to_grp(): return lax.all_to_all(x, 'grp', split_axis=0, concat_axis=0, tiled=True)  13.9 us
    ppermute x12, waiting for transfers between devices, shift(): return lax.ppermute(x, axis, [(i, (i + t) % count) for i in range(count)])  5.88 us
    all_to_all x2, waiting for transfers between devices, to_grp(): return lax.all_to_all(x, 'grp', split_axis=0, concat_axis=0, tiled=True)  5.13 us
    unnamed x30, local copies, waits for them, and re-layouts  4.4 us
    ppermute x3, starting transfers between devices, up(): lax.ppermute(tie(x, after), 'seq', [(i, i + 1) for i in range(step - 1, n...  3.85 us
  transfers between devices with their start and end apart: 17, of which 8 were waited for; matrix products, arithmetic and copies ran while one was open for 4% of the time, Pallas kernels for 14%

commit v1 on v0

--- a/solution.py
+++ b/solution.py
@@ -13,7 +13,6 @@
 MAX_IN_GROUP = 3
 SLOTS_R = 4
 NEGATIVE = -1e30
-LOG2E = 1.4426950408889634
 MIB = 1 << 20
 STREAM = 57
 
@@ -319,37 +318,12 @@
         )
 
 
-EXP2 = LOG2E / math.sqrt(HD)
+SCALE = 1.0 / math.sqrt(HD)
 
 
 def inverse_of(x):
     guess = pl.reciprocal(x, approx=True)
     return guess * (2.0 - x * guess)
-
-
-DEPTH = 30
-CUBIC = (0.99992498, 0.69583478, 0.22606662, 0.07802355)
-
-
-def power_of_two(x):
-    y = x + float(DEPTH)
-    whole = y.astype(jnp.int32)
-    rest = y - whole.astype(F32)
-    value = CUBIC[3] * 2.0**-DEPTH
-    for factor in reversed(CUBIC[:3]):
-        value = value * rest + factor * 2.0**-DEPTH
-    value = value * jnp.left_shift(jnp.ones_like(whole), whole).astype(F32)
-    return jnp.where(y < 0.0, 0.0, value)
-
-
-def by_products(count, t, half, odd):
-    if t == 1:
-        return True
-    if count == 2:
-        return False
-    if count == 3:
-        return t == 2 and half == 0 and odd
-    return t % 2 == 0 and t > 0 and half == 0
 
 
 def interleave(*tasks):
@@ -466,11 +440,7 @@
             def weight_step(at):
                 top = tops.pop(at)
                 for t, side in blocks(at):
-                    power = (part(at, t, side) - top) * EXP2
-                    if by_products(count, t, side, at // chunk % 2 == 1):
-                        weight = power_of_two(power)
-                    else:
-                        weight = jnp.exp2(power)
+                    weight = jnp.exp((part(at, t, side) - top) * SCALE)
                     lanes = slice(t * tokens + side * half, t * tokens + (side + 1) * half)
                     weights[slot][at : at + chunk, lanes] = weight.astype(BF16)
 

time: 147 us -> 138 us (0.939)
  the two profiles are of different devices: /device:TPU:27 before, /device:TPU:25 now
where the time goes in v1:
time: 138 us; the launch traced here: 137 us
  Pallas kernels  62.8 us (46%)
  starting transfers between devices  32.3 us (23%)
  blocking collectives  15.2 us (11%)
  waiting for transfers between devices  12.4 us (9%)
  other arithmetic  5.86 us (4%)
  local copies, waits for them, and re-layouts  5.59 us (4%)
  between operations  2.94 us (2%)
    pallas_call x9, Pallas kernels, call(): pl.pallas_call(body, out_shape=list(outs), grid_spec=pltpu.PrefetchScalar...  62.8 us
    ppermute x12, starting transfers between devices, shift(): return lax.ppermute(x, axis, [(i, (i + t) % count) for i in range(count)])  15.7 us
    all_to_all x1, blocking collectives, to_grp(): return lax.all_to_all(x, 'grp', split_axis=0, concat_axis=0, tiled=True)  15.2 us
    all_to_all x2, starting transfers between devices, to_grp(): return lax.all_to_all(x, 'grp', split_axis=0, concat_axis=0, tiled=True)  12.8 us
    all_to_all x2, waiting for transfers between devices, to_grp(): return lax.all_to_all(x, 'grp', split_axis=0, concat_axis=0, tiled=True)  7.08 us
    ppermute x12, waiting for transfers between devices, shift(): return lax.ppermute(x, axis, [(i, (i + t) % count) for i in range(count)])  5.3 us
    unnamed x30, local copies, waits for them, and re-layouts  4.4 us
    ppermute x3, starting transfers between devices, up(): lax.ppermute(tie(x, after), 'seq', [(i, i + 1) for i in range(step - 1, n...  3.85 us
  transfers between devices with their start and end apart: 17, of which 8 were waited for; matrix products, arithmetic and copies ran while one was open for 4% of the time, Pallas kernels for 14%

profile of v1, /device:TPU:25, one launch (start us, length us, event | category | flops | bytes accessed | tf_op | source)
XLA Modules:
  0.0 137.1 jit_solution(8433509624465147846)
XLA Ops:
  0.6 0.9 pad_maximum_fusion.new_ref
  1.5 0.7 pad_add_fusion.facts
  2.3 0.8 shard_map.149
  3.1 0.2 collective-permute-start.2
  3.3 3.1 %collective-permute-start = (bf16[4,2048]{1,0:T(4,128)(2,1)S(1)}, bf16[4,2048]{1,0:T(4,128)(2,1)S(1)}, u32[]{:S(2)}, u32[]{:S(2)}) collective-permute-start(bf16[4,2048]{1,0:T(4,128)(2,1)S(1)} %get-tuple-element.18.refs_0_), channel_id=1, source_target_pairs={{0,1},{1,2},{2,3},{3,0},{4,5},{5,6},{6,7},{7,4},{8,9},{9,10},{10,1... | collective-permute-start | bytes 49160 | tf_op jit(solution)/shard_map/ppermute | solution.py:547
  6.4 1.0 copy-done.1
  7.4 1.0 copy-done.2
  8.5 0.2 shard_map.150.refs_4_.refs_1_
  8.7 3.4 %shard_map.151 = (bf16[64,256]{1,0:T(8,128)(2,1)S(1)}, bf16[64,256]{1,0:T(8,128)(2,1)S(1)}, bf16[64,256]{1,0:T(8,128)(2,1)S(1)}, bf16[64,256]{1,0:T(8,128)(2,1)S(1)}) custom-call(s32[34]{0:T(128)S(1)} %pad_add_fusion.facts, bf16[4,2048]{1,0:T(4,128)(2,1)S(1)} %get-tuple-element.18.refs_0_, bf16[4,2048]{1,0:T(4,128)(2,1)S(1)} %collective-permute-done.refs_1_, ...), custom_call_target="tpu_custom_call" | custom-call | flops 33554432 | bytes 1245184 | tf_op jit(solution)/shard_map/pallas_call | solution.py:528
  12.1 0.7 collective-permute-start.3
  12.9 1.7 %collective-permute-start.4 = (bf16[64,256]{1,0:T(8,128)(2,1)S(1)}, bf16[64,256]{1,0:T(8,128)(2,1)S(1)}, u32[]{:S(2)}, u32[]{:S(2)}) collective-permute-start(bf16[64,256]{1,0:T(8,128)(2,1)S(1)} %get-tuple-element.21), channel_id=1, source_target_pairs={{0,2},{1,3},{2,0},{3,1},{4,6},{5,7},{6,4},{7,5},{8,10},{9,11},{10,... | collective-permute-start | bytes 98312 | tf_op jit(solution)/shard_map/ppermute | solution.py:547
  14.5 1.5 %collective-permute-start.5 = (bf16[64,256]{1,0:T(8,128)(2,1)S(1)}, bf16[64,256]{1,0:T(8,128)(2,1)S(1)}, u32[]{:S(2)}, u32[]{:S(2)}) collective-permute-start(bf16[64,256]{1,0:T(8,128)(2,1)S(1)} %get-tuple-element.22), channel_id=1, source_target_pairs={{0,1},{1,2},{2,3},{3,0},{4,5},{5,6},{6,7},{7,4},{8,9},{9,10},{10,1... | collective-permute-start | bytes 98312 | tf_op jit(solution)/shard_map/ppermute | solution.py:547
  16.0 0.8 collective-permute-done.3.refs_1_
  16.9 0.0 collective-permute-done.4.refs_2_
  16.9 0.4 collective-permute-done.5.refs_3_
  17.3 1.3 collective-permute-start.6
  18.6 0.9 shard_map.152
  19.5 7.5 %all-to-all-start = ((bf16[8,4,2048]{2,1,0:T(4,128)(2,1)}), bf16[8,4,2048]{2,1,0:T(4,128)(2,1)S(1)}, u32[]{:S(2)}, u32[]{:S(2)}) async-start(bf16[8,4,2048]{2,1,0:T(4,128)(2,1)} %shard_map.152), calls=%async_computation | async-start | bytes 262144 | tf_op jit(solution)/shard_map/all_to_all | solution.py:587
  27.0 0.9 select_reduce_fusion
  27.9 0.7 multiply_add_fusion
  28.6 0.7 fusion.1.pick_ref
  29.3 2.4 %all-to-all-done.parts_ref = bf16[8,4,2048]{2,1,0:T(4,128)(2,1)S(1)} async-done(((bf16[8,4,2048]{2,1,0:T(4,128)(2,1)}), bf16[8,4,2048]{2,1,0:T(4,128)(2,1)S(1)}, u32[]{:S(2)}, u32[]{:S(2)}) %all-to-all-start) | async-done | bytes 131104 | tf_op jit(solution)/shard_map/all_to_all | solution.py:587
  31.7 0.7 copy-done.5
  32.4 4.1 %shard_map.153.refs_0_ = bf16[16,1024]{1,0:T(8,128)(2,1)} custom-call(bf16[16,32]{1,0:T(8,128)(2,1)} %fusion.1.pick_ref, bf16[8,4,2048]{2,1,0:T(4,128)(2,1)} %copy-done.5, bf16[2048,1024]{1,0:T(8,128)(2,1)} %weight_ref.2), custom_call_target="tpu_custom_call" | custom-call | flops 67108864 | bytes 4359168 | tf_op jit(solution)/shard_map/pallas_call | solution.py:528
  36.5 2.4 %collective-permute-start.9 = (bf16[16,1024]{1,0:T(8,128)(2,1)}, bf16[16,1024]{1,0:T(8,128)(2,1)S(1)}, u32[]{:S(2)}, u32[]{:S(2)}) collective-permute-start(bf16[16,1024]{1,0:T(8,128)(2,1)} %shard_map.153.refs_0_), channel_id=1, source_target_pairs={{0,3},{1,0},{2,1},{3,2},{4,7},{5,4},{6,5},{7,6},{8,11},{9,8},{10,9... | collective-permute-start | bytes 98312 | tf_op jit(solution)/shard_map/ppermute | solution.py:547
  38.9 0.9 collective-permute-start.8
  39.8 1.5 %collective-permute-start.7 = (bf16[16,1024]{1,0:T(8,128)(2,1)}, bf16[16,1024]{1,0:T(8,128)(2,1)S(1)}, u32[]{:S(2)}, u32[]{:S(2)}) collective-permute-start(bf16[16,1024]{1,0:T(8,128)(2,1)} %shard_map.153.refs_0_), channel_id=1, source_target_pairs={{0,1},{1,2},{2,3},{3,0},{4,5},{5,6},{6,7},{7,4},{8,9},{9,10},{10,1... | collective-permute-start | bytes 98312 | tf_op jit(solution)/shard_map/ppermute | solution.py:547
  41.3 1.0 collective-permute-done.9.refs_3_
  42.3 1.3 collective-permute-done.8.refs_2_
  43.6 0.1 collective-permute-done.7.refs_1_
  43.8 1.3 collective-permute-start.10
  45.1 0.6 reshape.11.refs_5_
  45.7 7.8 %shard_map.154 = (f32[16,1024]{1,0:T(8,128)}, bf16[8,16,1152]{2,1,0:T(8,128)(2,1)}) custom-call(bf16[16,1024]{1,0:T(8,128)(2,1)} %shard_map.153.refs_0_, bf16[16,1024]{1,0:T(8,128)(2,1)} %copy-done.8, bf16[16,1024]{1,0:T(8,128)(2,1)} %copy-done.7, bf16[16,1024]{1,0:T(8,128)(2,1)} %copy-done.6, bf16[16,1024]{1,0:T(8,128)(2,1)} %refs_4_.1, ...), custom_call_target="tpu_custom_call" | custom-call | flops 268435456 | bytes 17303552 | tf_op jit(solution)/shard_map/pallas_call | solution.py:528
  53.6 15.2 %all_to_all.15.parts_ref = bf16[8,16,1152]{2,1,0:T(8,128)(2,1)S(1)} all-to-all(bf16[8,16,1152]{2,1,0:T(8,128)(2,1)} %get-tuple-element.27), channel_id=1, replica_groups=mesh['grp'=8,'seq'=4] {'grp'}, dimensions={0} | all-to-all | bytes 589824 | tf_op jit(solution)/shard_map/all_to_all | solution.py:587
  68.8 0.8 shard_map.155
  69.6 1.3 collective-permute-start.11
  70.9 5.2 %all-to-all-start.2 = ((bf16[8,16,512]{2,1,0:T(8,128)(2,1)}), bf16[8,16,512]{2,1,0:T(8,128)(2,1)S(1)}, u32[]{:S(2)}, u32[]{:S(2)}) async-start(bf16[8,16,512]{2,1,0:T(8,128)(2,1)} %shard_map.155), calls=%async_computation.2 | async-start | bytes 262144 | tf_op jit(solution)/shard_map/all_to_all | solution.py:587
  76.1 4.7 %all-to-all-done.2.parts_ref = bf16[8,16,512]{2,1,0:T(8,128)(2,1)S(1)} async-done(((bf16[8,16,512]{2,1,0:T(8,128)(2,1)}), bf16[8,16,512]{2,1,0:T(8,128)(2,1)S(1)}, u32[]{:S(2)}, u32[]{:S(2)}) %all-to-all-start.2) | async-done | bytes 131104 | tf_op jit(solution)/shard_map/all_to_all | solution.py:587
  80.8 0.7 copy-done.4
  81.5 5.9 %shard_map.157 = (f32[16,256]{1,0:T(8,128)}, f32[16,256]{1,0:T(8,128)}, f32[16,256]{1,0:T(8,128)}, f32[16,256]{1,0:T(8,128)}) custom-call(s32[34]{0:T(128)} %copy-done.3, bf16[8,16,512]{2,1,0:T(8,128)(2,1)} %copy-done.4, bf16[4096,1024]{1,0:T(8,128)(2,1)} %weight_ref.3), custom_call_target="tpu_custom_call" | custom-call | flops 134217728 | bytes 8585216 | tf_op jit(solution)/shard_map/pallas_call | solution.py:528
  87.4 0.1 collective-permute-start.12
  87.5 3.6 %collective-permute-start.13 = (f32[16,256]{1,0:T(8,128)}, f32[16,256]{1,0:T(8,128)S(1)}, u32[]{:S(2)}, u32[]{:S(2)}) collective-permute-start(f32[16,256]{1,0:T(8,128)} %get-tuple-element.32), channel_id=1, source_target_pairs={{0,2},{1,3},{2,0},{3,1},{4,6},{5,7},{6,4},{7,5},{8,10},{9,11},{10,... | collective-permute-start | bytes 49160 | tf_op jit(solution)/shard_map/ppermute | solution.py:547
  91.1 0.6 fusion.2
  93.7 0.6 concatenate.12.facts
  94.2 1.6 %collective-permute-done.12 = f32[16,256]{1,0:T(8,128)S(1)} collective-permute-done((f32[16,256]{1,0:T(8,128)}, f32[16,256]{1,0:T(8,128)S(1)}, u32[]{:S(2)}, u32[]{:S(2)}) %collective-permute-start.12) | collective-permute-done | bytes 16416 | tf_op jit(solution)/shard_map/ppermute | solution.py:547
  95.8 1.3 add_convert_fusion
  97.2 1.0 copy-done.14
  98.2 38.8 %shard_map.156 = bf16[256,8192]{1,0:T(8,128)(2,1)} custom-call(s32[35]{0:T(128)} %concatenate.12.facts, bf16[256,8192]{1,0:T(8,128)(2,1)} %refs_0_.1, bf16[2048,256]{1,0:T(8,128)(2,1)} %copy-done, bf16[2048,256]{1,0:T(8,128)(2,1)} %copy-done.12, bf16[2048,256]{1,0:T(8,128)(2,1)} %copy-done.13, bf16[2048,256]{1,0:T(8,128)(2,1)} %copy-done.14), custom_call_target="tpu_custom_call" | custom-call | flops 17179869184 | bytes 12582912 | tf_op jit(solution)/shard_map/pallas_call | solution.py:528
  (35 shorter events, 0.1 us)
Async XLA Ops:
  0.6 44.5 %copy-start.11 = (bf16[1024]{0:T(1024)(128)(2,1)S(1)}, bf16[1024]{0:T(1024)(128)(2,1)}, u32[]{:S(2)}) copy-start(bf16[1024]{0:T(1024)(128)(2,1)} %param.24) | copy-start | bytes 6148
  2.3 51.3 %copy-start.3 = (s32[34]{0:T(128)}, s32[34]{0:T(128)S(1)}, u32[]{:S(2)}) copy-start(s32[34]{0:T(128)S(1)} %pad_add_fusion.facts) | copy-start | bytes 412
  3.1 5.6 %collective-permute-start.2 = (bf16[4,2048]{1,0:T(4,128)(2,1)S(1)}, bf16[4,2048]{1,0:T(4,128)(2,1)S(1)}, u32[]{:S(2)}, u32[]{:S(2)}) collective-permute-start(bf16[4,2048]{1,0:T(4,128)(2,1)S(1)} %get-tuple-element.18.refs_0_), channel_id=1, source_target_pairs={{0,3},{1,0},{2,1},{3,2},{4,7},{5,4},{6,5},{7,6},{8,11},{9,8},{10,9... | collective-permute-start | bytes 49160 | tf_op jit(solution)/shard_map/ppermute | solution.py:547
  3.3 5.4 %collective-permute-start.1 = (bf16[4,2048]{1,0:T(4,128)(2,1)S(1)}, bf16[4,2048]{1,0:T(4,128)(2,1)S(1)}, u32[]{:S(2)}, u32[]{:S(2)}) collective-permute-start(bf16[4,2048]{1,0:T(4,128)(2,1)S(1)} %get-tuple-element.18.refs_0_), channel_id=1, source_target_pairs={{0,2},{1,3},{2,0},{3,1},{4,6},{5,7},{6,4},{7,5},{8,10},{9,11},{10,... | collective-permute-start | bytes 49160 | tf_op jit(solution)/shard_map/ppermute | solution.py:547
  3.3 5.4 %collective-permute-start = (bf16[4,2048]{1,0:T(4,128)(2,1)S(1)}, bf16[4,2048]{1,0:T(4,128)(2,1)S(1)}, u32[]{:S(2)}, u32[]{:S(2)}) collective-permute-start(bf16[4,2048]{1,0:T(4,128)(2,1)S(1)} %get-tuple-element.18.refs_0_), channel_id=1, source_target_pairs={{0,1},{1,2},{2,3},{3,0},{4,5},{5,6},{6,7},{7,4},{8,9},{9,10},{10,1... | collective-permute-start | bytes 49160 | tf_op jit(solution)/shard_map/ppermute | solution.py:547
  6.4 1.0 copy-start.1
  7.4 1.0 copy-start.2
  8.7 44.9 %copy-start = (bf16[2048,256]{1,0:T(8,128)(2,1)}, bf16[2048,256]{1,0:T(8,128)(2,1)S(1)}, u32[]{:S(2)}) copy-start(bf16[2048,256]{1,0:T(8,128)(2,1)S(1)} %shard_map.150.refs_4_.refs_1_) | copy-start | bytes 3145732
  12.1 4.7 %collective-permute-start.3 = (bf16[64,256]{1,0:T(8,128)(2,1)S(1)}, bf16[64,256]{1,0:T(8,128)(2,1)S(1)}, u32[]{:S(2)}, u32[]{:S(2)}) collective-permute-start(bf16[64,256]{1,0:T(8,128)(2,1)S(1)} %get-tuple-element.20), channel_id=1, source_target_pairs={{0,3},{1,0},{2,1},{3,2},{4,7},{5,4},{6,5},{7,6},{8,11},{9,8},{10,9... | collective-permute-start | bytes 98312 | tf_op jit(solution)/shard_map/ppermute | solution.py:547
  12.9 4.0 %collective-permute-start.4 = (bf16[64,256]{1,0:T(8,128)(2,1)S(1)}, bf16[64,256]{1,0:T(8,128)(2,1)S(1)}, u32[]{:S(2)}, u32[]{:S(2)}) collective-permute-start(bf16[64,256]{1,0:T(8,128)(2,1)S(1)} %get-tuple-element.21), channel_id=1, source_target_pairs={{0,2},{1,3},{2,0},{3,1},{4,6},{5,7},{6,4},{7,5},{8,10},{9,11},{10,... | collective-permute-start | bytes 98312 | tf_op jit(solution)/shard_map/ppermute | solution.py:547
  14.5 2.8 %collective-permute-start.5 = (bf16[64,256]{1,0:T(8,128)(2,1)S(1)}, bf16[64,256]{1,0:T(8,128)(2,1)S(1)}, u32[]{:S(2)}, u32[]{:S(2)}) collective-permute-start(bf16[64,256]{1,0:T(8,128)(2,1)S(1)} %get-tuple-element.22), channel_id=1, source_target_pairs={{0,1},{1,2},{2,3},{3,0},{4,5},{5,6},{6,7},{7,4},{8,9},{9,10},{10,1... | collective-permute-start | bytes 98312 | tf_op jit(solution)/shard_map/ppermute | solution.py:547
  17.3 26.5 %collective-permute-start.6 = (bf16[2048,256]{1,0:T(8,128)(2,1)S(1)}, bf16[2048,256]{1,0:T(8,128)(2,1)S(1)}, u32[]{:S(2)}, u32[]{:S(2)}) collective-permute-start(bf16[2048,256]{1,0:T(8,128)(2,1)S(1)} %shard_map.150.refs_4_.refs_1_), channel_id=1, source_target_pairs={{0,1},{1,2},{2,3},{4,5},{5,6},{6,7},{8,9},{9,10},{10,11},{12,13},{... | collective-permute-start | bytes 3145736 | tf_op jit(solution)/shard_map/ppermute | solution.py:593
  19.5 12.2 %all-to-all-start = ((bf16[8,4,2048]{2,1,0:T(4,128)(2,1)}), bf16[8,4,2048]{2,1,0:T(4,128)(2,1)S(1)}, u32[]{:S(2)}, u32[]{:S(2)}) async-start(bf16[8,4,2048]{2,1,0:T(4,128)(2,1)} %shard_map.152), calls=%async_computation | async-start | bytes 262144 | tf_op jit(solution)/shard_map/all_to_all | solution.py:587
  31.7 0.7 copy-start.5
  36.5 5.8 %collective-permute-start.9 = (bf16[16,1024]{1,0:T(8,128)(2,1)}, bf16[16,1024]{1,0:T(8,128)(2,1)S(1)}, u32[]{:S(2)}, u32[]{:S(2)}) collective-permute-start(bf16[16,1024]{1,0:T(8,128)(2,1)} %shard_map.153.refs_0_), channel_id=1, source_target_pairs={{0,3},{1,0},{2,1},{3,2},{4,7},{5,4},{6,5},{7,6},{8,11},{9,8},{10,9... | collective-permute-start | bytes 98312 | tf_op jit(solution)/shard_map/ppermute | solution.py:547
  38.9 4.7 %collective-permute-start.8 = (bf16[16,1024]{1,0:T(8,128)(2,1)}, bf16[16,1024]{1,0:T(8,128)(2,1)S(1)}, u32[]{:S(2)}, u32[]{:S(2)}) collective-permute-start(bf16[16,1024]{1,0:T(8,128)(2,1)} %shard_map.153.refs_0_), channel_id=1, source_target_pairs={{0,2},{1,3},{2,0},{3,1},{4,6},{5,7},{6,4},{7,5},{8,10},{9,11},{10,... | collective-permute-start | bytes 98312 | tf_op jit(solution)/shard_map/ppermute | solution.py:547
  39.8 4.0 %collective-permute-start.7 = (bf16[16,1024]{1,0:T(8,128)(2,1)}, bf16[16,1024]{1,0:T(8,128)(2,1)S(1)}, u32[]{:S(2)}, u32[]{:S(2)}) collective-permute-start(bf16[16,1024]{1,0:T(8,128)(2,1)} %shard_map.153.refs_0_), channel_id=1, source_target_pairs={{0,1},{1,2},{2,3},{3,0},{4,5},{5,6},{6,7},{7,4},{8,9},{9,10},{10,1... | collective-permute-start | bytes 98312 | tf_op jit(solution)/shard_map/ppermute | solution.py:547
  42.3 3.4 %copy-start.6 = (bf16[16,1024]{1,0:T(8,128)(2,1)}, bf16[16,1024]{1,0:T(8,128)(2,1)S(1)}, u32[]{:S(2)}) copy-start(bf16[16,1024]{1,0:T(8,128)(2,1)S(1)} %collective-permute-done.9.refs_3_) | copy-start | bytes 98308
  43.6 2.1 %copy-start.7 = (bf16[16,1024]{1,0:T(8,128)(2,1)}, bf16[16,1024]{1,0:T(8,128)(2,1)S(1)}, u32[]{:S(2)}) copy-start(bf16[16,1024]{1,0:T(8,128)(2,1)S(1)} %collective-permute-done.8.refs_2_) | copy-start | bytes 98308
  43.8 1.9 %copy-start.8 = (bf16[16,1024]{1,0:T(8,128)(2,1)}, bf16[16,1024]{1,0:T(8,128)(2,1)S(1)}, u32[]{:S(2)}) copy-start(bf16[16,1024]{1,0:T(8,128)(2,1)S(1)} %collective-permute-done.7.refs_1_) | copy-start | bytes 98308
  43.8 9.8 %copy-start.12 = (bf16[2048,256]{1,0:T(8,128)(2,1)}, bf16[2048,256]{1,0:T(8,128)(2,1)S(1)}, u32[]{:S(2)}) copy-start(bf16[2048,256]{1,0:T(8,128)(2,1)S(1)} %collective-permute-done.6.refs_2_) | copy-start | bytes 3145732
  43.8 25.8 %collective-permute-start.10 = (bf16[2048,256]{1,0:T(8,128)(2,1)S(1)}, bf16[2048,256]{1,0:T(8,128)(2,1)S(1)}, u32[]{:S(2)}, u32[]{:S(2)}) collective-permute-start(bf16[2048,256]{1,0:T(8,128)(2,1)S(1)} %collective-permute-done.6.refs_2_), channel_id=1, source_target_pairs={{1,2},{2,3},{5,6},{6,7},{9,10},{10,11},{13,14},{14,15},{17,18},{18... | collective-permute-start | bytes 3145736 | tf_op jit(solution)/shard_map/ppermute | solution.py:593
  53.6 37.5 %copy-start.9 = (s32[16]{0:T(128)S(1)}, s32[16]{0:T(128)}, u32[]{:S(2)}) copy-start(s32[16]{0:T(128)} %param.15) | copy-start | bytes 196
  53.6 37.5 %copy-start.10 = (s32[16]{0:T(128)S(1)}, s32[16]{0:T(128)}, u32[]{:S(2)}) copy-start(s32[16]{0:T(128)} %param.14) | copy-start | bytes 196
  69.6 27.6 %copy-start.13 = (bf16[2048,256]{1,0:T(8,128)(2,1)}, bf16[2048,256]{1,0:T(8,128)(2,1)S(1)}, u32[]{:S(2)}) copy-start(bf16[2048,256]{1,0:T(8,128)(2,1)S(1)} %collective-permute-done.10.refs_3_) | copy-start | bytes 3145732
  69.6 27.6 %collective-permute-start.11 = (bf16[2048,256]{1,0:T(8,128)(2,1)S(1)}, bf16[2048,256]{1,0:T(8,128)(2,1)S(1)}, u32[]{:S(2)}, u32[]{:S(2)}) collective-permute-start(bf16[2048,256]{1,0:T(8,128)(2,1)S(1)} %collective-permute-done.10.refs_3_), channel_id=1, source_target_pairs={{2,3},{6,7},{10,11},{14,15},{18,19},{22,23},{26,27},{30,31}} | collective-permute-start | bytes 3145736 | tf_op jit(solution)/shard_map/ppermute | solution.py:593
  70.9 9.9 %all-to-all-start.2 = ((bf16[8,16,512]{2,1,0:T(8,128)(2,1)}), bf16[8,16,512]{2,1,0:T(8,128)(2,1)S(1)}, u32[]{:S(2)}, u32[]{:S(2)}) async-start(bf16[8,16,512]{2,1,0:T(8,128)(2,1)} %shard_map.155), calls=%async_computation.2 | async-start | bytes 262144 | tf_op jit(solution)/shard_map/all_to_all | solution.py:587
  80.8 0.7 copy-start.4
  87.4 8.4 %collective-permute-start.12 = (f32[16,256]{1,0:T(8,128)}, f32[16,256]{1,0:T(8,128)S(1)}, u32[]{:S(2)}, u32[]{:S(2)}) collective-permute-start(f32[16,256]{1,0:T(8,128)} %get-tuple-element.31), channel_id=1, source_target_pairs={{0,1},{1,2},{2,3},{3,0},{4,5},{5,6},{6,7},{7,4},{8,9},{9,10},{10,1... | collective-permute-start | bytes 49160 | tf_op jit(solution)/shard_map/ppermute | solution.py:547
  87.5 8.4 %collective-permute-start.13 = (f32[16,256]{1,0:T(8,128)}, f32[16,256]{1,0:T(8,128)S(1)}, u32[]{:S(2)}, u32[]{:S(2)}) collective-permute-start(f32[16,256]{1,0:T(8,128)} %get-tuple-element.32), channel_id=1, source_target_pairs={{0,2},{1,3},{2,0},{3,1},{4,6},{5,7},{6,4},{7,5},{8,10},{9,11},{10,... | collective-permute-start | bytes 49160 | tf_op jit(solution)/shard_map/ppermute | solution.py:547
  91.1 4.8 %collective-permute-start.14 = (f32[16,256]{1,0:T(8,128)}, f32[16,256]{1,0:T(8,128)S(1)}, u32[]{:S(2)}, u32[]{:S(2)}) collective-permute-start(f32[16,256]{1,0:T(8,128)} %get-tuple-element.33), channel_id=1, source_target_pairs={{0,3},{1,0},{2,1},{3,2},{4,7},{5,4},{6,5},{7,6},{8,11},{9,8},{10,9... | collective-permute-start | bytes 49160 | tf_op jit(solution)/shard_map/ppermute | solution.py:547
  97.2 1.0 copy-start.14
